TPU v7x, 32 devices: a whole 2x2x4 slice. The times are simulated.
32 devices in a mesh: row: 4 (over z), col: 8 (over y, x, core).
Axes of the slice: x: 2, y: 2, z: 4, core: 2. Of those that a mesh axis runs over, the one named last changes fastest.
Arguments:
- points: bfloat16 [3, 12288], P(None, ('row', 'col')), as said below
- omega: bfloat16 [64, 12288], P(None, ('row', 'col')), may hold values from -6 to 6
- leaf_extra: int32 [32], replicated, may hold values from 1 to 769, 4128 in all
- owner_map: int32 [32], replicated, may hold values from 0 to 31, as said below
Outputs:
- samples: bfloat16 [64, 12288], P(None, ('row', 'col'))
- coupled: float32 [64, 4096], P(('row', 'col'))
Inputs may be any that keep to these rules, and one draw needn't show every extreme that they name: `leaf_extra`: the values sum to 4128, and the largest is reached in every draw. `owner_map`: exactly 16 devices own 2 leaves each; the other devices own none. All coordinates lie in [0, 1]; the points fill the unit cube and are numbered in cluster tree order, so that points with near numbers lie near one another.
All inputs are finite; a program needn't handle non-finite values.
Results may differ from a plain program's by a relative error of at most 0.0037.
Values may be sent and summed in bfloat16 or wider, within the bound.
A program may use at most 128 MiB of HBM per device.

v0:
```python
import math

import jax
import jax.numpy as jnp
from jax import lax
from jax.sharding import PartitionSpec as P

LEAF_MIN = 256
LEAF_MAX = 1024
SLOTS = 2


GAMMA = 8.0
SHIFT = 1.0
AMPC = 4.0


def kernel_tile(col_pts, row_pts, amp):
    first = col_pts[0][:, None] - row_pts[0][None, :]
    second = col_pts[1][:, None] - row_pts[1][None, :]
    third = col_pts[2][:, None] - row_pts[2][None, :]
    dist = first * first + second * second + third * third
    return amp * jnp.exp(-GAMMA * dist)


def lower_triangular_solver(factor, rhs, flip):
    return lax.linalg.triangular_solve(factor, rhs, left_side=True, lower=True, transpose_a=flip)


def block_of(length, limit):
    return length if length <= limit else math.gcd(length, limit)


def accumulate(row_pts, amp, carry, pieces):
    col_pts, col_omega = pieces
    rows = row_pts.shape[1]
    row_blk = block_of(rows, 1024)
    col_blk = block_of(col_pts.shape[1], 2048)

    def col_step(outer, acc):
        cpts = lax.dynamic_slice_in_dim(col_pts, outer * col_blk, col_blk, 1).astype(jnp.float32)
        comega = lax.dynamic_slice_in_dim(col_omega, outer * col_blk, col_blk, 1)

        def row_step(inner, acc_inner):
            tile = kernel_tile(cpts, row_pts, amp).astype(jnp.bfloat16)
            term = jnp.dot(comega, tile, preferred_element_type=jnp.float32)
            return acc_inner + term

        return lax.fori_loop(0, rows // row_blk, row_step, acc)

    return lax.fori_loop(0, col_pts.shape[1] // col_blk, col_step, carry)


def coupling(ys, leaf_pts, valid, live, amp, ranks):
    eye_r = jnp.eye(ranks, dtype=jnp.float32)
    gram = jnp.dot(ys, ys.T, precision=lax.Precision.HIGHEST)
    gram = jnp.where(live, gram, eye_r)
    chol_g = jnp.linalg.cholesky(gram)
    basis_transposed = lower_triangular_solver(chol_g, ys, False)
    width = ys.shape[1]
    inner = jnp.where(valid[:, None] & valid[None, :], kernel_tile(leaf_pts, leaf_pts, amp), 0.0)
    dmat = inner + SHIFT * jnp.eye(width, dtype=jnp.float32)
    diagonal_cholesky_factor = jnp.linalg.cholesky(dmat)
    value_matrix = lower_triangular_solver(diagonal_cholesky_factor, basis_transposed.T, False)
    middle_matrix = jnp.dot(value_matrix.T, value_matrix, precision=lax.Precision.HIGHEST)
    middle_matrix = jnp.where(live, middle_matrix, eye_r)
    chol_m = jnp.linalg.cholesky(middle_matrix)
    halfway = lower_triangular_solver(chol_m, eye_r, False)
    inverse = lower_triangular_solver(chol_m, halfway, True)
    return jnp.where(live, inverse, 0.0).reshape(ranks * ranks)


def shards(points, omega, leaf_extra, owner_map):
    per_dev = points.shape[1]
    ranks = omega.shape[0]
    n_all = per_dev * lax.axis_size("row") * lax.axis_size("col")
    amp = AMPC / math.sqrt(n_all)
    own_pts = points.astype(jnp.float32)
    empty = jnp.zeros((ranks, per_dev), jnp.float32)
    total = accumulate(
        own_pts,
        amp,
        empty,
        (
            lax.all_gather(points, ("row", "col"), axis=1, tiled=True),
            lax.all_gather(omega, ("row", "col"), axis=1, tiled=True),
        ),
    )
    samples = (total + SHIFT * omega.astype(jnp.float32)).astype(jnp.bfloat16)
    device = lax.axis_index(("row", "col"))
    sizes = leaf_extra + (LEAF_MIN - 1)
    starts = jnp.cumsum(sizes) - sizes
    offsets = jnp.arange(LEAF_MAX, dtype=jnp.int32)
    vmapped = jax.vmap(coupling, in_axes=(0, 0, 0, 0, None, None))
    mine = owner_map == device
    order = jnp.cumsum(mine.astype(jnp.int32)) - 1
    slot_ids = jnp.arange(SLOTS, dtype=jnp.int32)
    picked = (mine[None, :] & (order[None, :] == slot_ids[:, None])).astype(jnp.int32)
    slot_start = jnp.sum(picked * starts[None, :], axis=1)
    slot_size = jnp.sum(picked * sizes[None, :], axis=1)
    live = jnp.sum(picked, axis=1) > 0
    wanted = (slot_start[:, None] + offsets[None, :]).reshape(SLOTS * LEAF_MAX)
    valid = offsets[None, :] < slot_size[:, None]
    inside = valid.reshape(SLOTS * LEAF_MAX)
    init = (
        jnp.zeros((3, SLOTS * LEAF_MAX), jnp.bfloat16),
        jnp.zeros((ranks, SLOTS * LEAF_MAX), jnp.bfloat16),
    )
    piece_pts = lax.all_gather(points, ("row", "col"), axis=1, tiled=True)
    piece_samp = lax.all_gather(samples, ("row", "col"), axis=1, tiled=True)
    length = piece_pts.shape[1]
    hit = inside & (wanted >= 0) & (wanted < length)
    spot = jnp.clip(wanted, 0, length - 1)
    new_pts = jnp.where(hit[None, :], jnp.take(piece_pts, spot, axis=1), init[0])
    new_samp = jnp.where(hit[None, :], jnp.take(piece_samp, spot, axis=1), init[1])
    slot_points = jnp.transpose(new_pts.astype(jnp.float32).reshape(3, SLOTS, LEAF_MAX), (1, 0, 2))
    slot_samp = jnp.transpose(
        new_samp.astype(jnp.float32).reshape(ranks, SLOTS, LEAF_MAX), (1, 0, 2)
    )
    couplings = vmapped(slot_samp, slot_points, valid, live, amp, ranks)
    return (samples, couplings)


def solution(mesh):
    return jax.shard_map(
        shards,
        mesh=mesh,
        in_specs=(P(None, ("row", "col")), P(None, ("row", "col")), P(), P()),
        out_specs=(P(None, ("row", "col")), P(("row", "col"), None)),
        check_vma=False,
    )
```

profile of v0, /device:TPU:0, one launch (start us, length us, event | category | flops | bytes accessed | tf_op | source)
XLA Modules:
  0.0 781.8 jit_solution(15440192247602807251)
XLA Ops:
  12.5 55.7 %all_gather.11 = bf16[3,12288]{0,1:T(8,128)(2,1)S(1)} all-gather(bf16[3,384]{0,1:T(8,128)(2,1)S(1)} %copy.80), channel_id=1, replica_groups=mesh['row'=4,'col'=8] {'row','col'}, dimensions={1}, use_global_device_ids=true | all-gather | bytes 76032 | tf_op jit(solution)/shard_map/all_gather | solution.py:85
  78.9 10.7 %fusion.8 = f32[2,1024,1024]{2,1,0:T(8,128)S(1)} fusion(f32[1024,1024]{1,0:T(8,128)} %get-tuple-element.262, f32[1024,1024]{1,0:T(8,128)} %get-tuple-element.261, f32[2,1024]{1,0:T(2,128)S(1)} %get-tuple-element.248, f32[2,1024]{1,0:T(2,128)S(1)} %get-tuple-element.249, f32[2,1024]{1,0:T(2,128)S(1)} %get-tuple-element.247, ...), kind=kLoop, calls=%fused_computation.19 | loop fusion | flops 56623104 | bytes 16803840 | tf_op jit(solution)/shard_map/vmap(jit(cholesky))/div | solution.py:63
  92.9 23.5 %custom-call.81 = f32[2,128,128]{2,1,0:T(8,128)S(1)} custom-call(f32[2,128,128]{2,1,0:T(8,128)S(1)} %cholesky.640), custom_call_target="Cholesky" | custom-call | tf_op jit(solution)/shard_map/vmap(jit(cholesky))/cholesky | solution.py:63
  120.6 19.7 %custom-call.82 = f32[2,1,128,128]{2,3,1,0:T(8,128)S(1)} custom-call(f32[2,1,128,128]{3,2,1,0:T(8,128)S(1)} %select_bitcast_fusion.6), custom_call_target="InvertDiagBlocksLowerTriangular" | custom-call | tf_op jit(solution)/shard_map/vmap(jit(cholesky))/cholesky | solution.py:63
  146.5 23.9 %custom-call.83 = f32[2,128,128]{2,1,0:T(8,128)S(1)} custom-call(f32[2,128,128]{2,1,0:T(8,128)S(1)} %cholesky.644), custom_call_target="Cholesky" | custom-call | tf_op jit(solution)/shard_map/vmap(jit(cholesky))/cholesky | solution.py:63
  171.1 20.3 %custom-call.84 = f32[2,1,128,128]{2,3,1,0:T(8,128)} custom-call(f32[2,1,128,128]{3,2,1,0:T(8,128)S(1)} %get-tuple-element.220), custom_call_target="InvertDiagBlocksLowerTriangular" | custom-call | tf_op jit(solution)/shard_map/vmap(jit(cholesky))/cholesky | solution.py:63
  198.4 23.6 %custom-call.85 = f32[2,128,128]{2,1,0:T(8,128)S(1)} custom-call(f32[2,128,128]{2,1,0:T(8,128)S(1)} %cholesky.649), custom_call_target="Cholesky" | custom-call | tf_op jit(solution)/shard_map/vmap(jit(cholesky))/cholesky | solution.py:63
  222.7 20.3 %custom-call.86 = f32[2,1,128,128]{2,3,1,0:T(8,128)} custom-call(f32[2,1,128,128]{3,2,1,0:T(8,128)S(1)} %get-tuple-element.218), custom_call_target="InvertDiagBlocksLowerTriangular" | custom-call | tf_op jit(solution)/shard_map/vmap(jit(cholesky))/cholesky | solution.py:63
  251.0 24.5 %custom-call.87 = f32[2,128,128]{2,1,0:T(8,128)S(1)} custom-call(f32[2,128,128]{2,1,0:T(8,128)} %cholesky.654), custom_call_target="Cholesky" | custom-call | tf_op jit(solution)/shard_map/vmap(jit(cholesky))/cholesky | solution.py:63
  276.2 21.1 %custom-call.88 = f32[2,1,128,128]{2,3,1,0:T(8,128)} custom-call(f32[2,1,128,128]{3,2,1,0:T(8,128)} %get-tuple-element.216), custom_call_target="InvertDiagBlocksLowerTriangular" | custom-call | tf_op jit(solution)/shard_map/vmap(jit(cholesky))/cholesky | solution.py:63
  305.1 24.3 %custom-call.89 = f32[2,128,128]{2,1,0:T(8,128)S(1)} custom-call(f32[2,128,128]{2,1,0:T(8,128)} %cholesky.659), custom_call_target="Cholesky" | custom-call | tf_op jit(solution)/shard_map/vmap(jit(cholesky))/cholesky | solution.py:63
  330.1 21.5 %custom-call.90 = f32[2,1,128,128]{2,3,1,0:T(8,128)} custom-call(f32[2,1,128,128]{3,2,1,0:T(8,128)} %get-tuple-element.214), custom_call_target="InvertDiagBlocksLowerTriangular" | custom-call | tf_op jit(solution)/shard_map/vmap(jit(cholesky))/cholesky | solution.py:63
  358.2 24.9 %custom-call.91 = f32[2,128,128]{2,1,0:T(8,128)} custom-call(f32[2,128,128]{2,1,0:T(8,128)} %cholesky.664), custom_call_target="Cholesky" | custom-call | tf_op jit(solution)/shard_map/vmap(jit(cholesky))/cholesky | solution.py:63
  384.8 21.2 %custom-call.92 = f32[2,1,128,128]{2,3,1,0:T(8,128)} custom-call(f32[2,1,128,128]{3,2,1,0:T(8,128)} %get-tuple-element.212), custom_call_target="InvertDiagBlocksLowerTriangular" | custom-call | tf_op jit(solution)/shard_map/vmap(jit(cholesky))/cholesky | solution.py:63
  411.9 24.9 %custom-call.93 = f32[2,128,128]{2,1,0:T(8,128)} custom-call(f32[2,128,128]{2,1,0:T(8,128)} %cholesky.669), custom_call_target="Cholesky" | custom-call | tf_op jit(solution)/shard_map/vmap(jit(cholesky))/cholesky | solution.py:63
  442.1 20.5 %custom-call.94 = f32[2,1,128,128]{2,3,1,0:T(8,128)S(1)} custom-call(f32[2,1,128,128]{3,2,1,0:T(8,128)} %get-tuple-element.210), custom_call_target="InvertDiagBlocksLowerTriangular" | custom-call | tf_op jit(solution)/shard_map/vmap(jit(cholesky))/cholesky | solution.py:63
  466.1 23.7 %custom-call.95 = f32[2,128,128]{2,1,0:T(8,128)S(1)} custom-call(f32[2,128,128]{2,1,0:T(8,128)S(1)} %convolution_subtract_fusion.1), custom_call_target="Cholesky" | custom-call | tf_op jit(solution)/shard_map/vmap(jit(cholesky))/cholesky | solution.py:63
  502.0 20.0 %while.24 = (s32[]{:T(128)}, f32[64,384]{1,0:T(8,128)S(1)}, bf16[64,12288]{1,0:T(8,128)(2,1)}, bf16[3,12288]{1,0:T(4,128)(2,1)}, f32[3,384]{1,0:T(4,128)S(1)}, /*index=5*/s32[]{:T(128)}, s32[]{:T(128)}, s32[]{:T(128)}, s32[]{:T(128)}) while((s32[]{:T(128)}, f32[64,384]{1,0:T(8,128)S(1)}, bf16[64,12288]{1,0:T(8,128)(2,1)}, ...), condition=%wide.region_1.2_spmd.clone, body=%wide.region_0.1_spmd.clone.sunk | while | flops 109369352 | bytes 583333 | solution.py:51
  522.9 23.2 %while.23 = (s32[]{:T(128)}, f32[2,1024,1024]{2,1,0:T(8,128)}, s32[8,2]{0,1:T(2,128)S(1)}, f32[8,2,128,128]{3,2,0,1:T(8,128)S(1)}, s32[]{:T(128)}) while((s32[]{:T(128)}, f32[2,1024,1024]{2,1,0:T(8,128)}, s32[8,2]{0,1:T(2,128)S(1)}, f32[8,2,128,128]{3,2,0,1:T(8,128)S(1)}, s32[]{:T(128)}) %tuple.118), condition=%wide.while_cond, body=%wide.while_body.sunk | while | flops 2 | bytes 262261 | solution.py:27
  546.0 157.2 %custom-call.96 = f32[2,8,128,128]{2,3,1,0:T(8,128)S(1)} custom-call(f32[2,8,128,128]{3,2,1,0:T(8,128)S(1)} %bitcast.187), custom_call_target="InvertDiagBlocksLowerTriangular" | custom-call | tf_op jit(solution)/shard_map/vmap()/triangular_solve | solution.py:27
  713.4 12.0 %custom-call.101 = f32[2,64,64]{2,1,0:T(8,128)S(1)} custom-call(f32[2,64,64]{2,1,0:T(8,128)S(1)} %copy.104), custom_call_target="Cholesky" | custom-call | tf_op jit(solution)/shard_map/vmap(jit(cholesky))/cholesky | solution.py:58
  725.7 9.8 %custom-call.97 = f32[2,1,64,64]{2,3,1,0:T(8,128)S(1)} custom-call(f32[2,1,64,64]{3,2,1,0:T(8,128)S(1)} %fusion.104), custom_call_target="InvertDiagBlocksLowerTriangular" | custom-call | tf_op jit(solution)/shard_map/vmap()/triangular_solve | solution.py:27
  751.5 11.7 %custom-call.102 = f32[2,64,64]{2,1,0:T(8,128)S(1)} custom-call(f32[2,64,64]{2,1,0:T(8,128)S(1)} %copy.116), custom_call_target="Cholesky" | custom-call | tf_op jit(solution)/shard_map/vmap(jit(cholesky))/cholesky | solution.py:67
  763.4 9.8 %custom-call.98 = f32[2,1,64,64]{2,3,1,0:T(8,128)S(1)} custom-call(f32[2,1,64,64]{3,2,1,0:T(8,128)S(1)} %fusion.103), custom_call_target="InvertDiagBlocksLowerTriangular" | custom-call | tf_op jit(solution)/shard_map/vmap()/triangular_solve | solution.py:27
  (211 shorter events, 161.5 us)
Async XLA Ops:
  7.2 5.1 copy-start.18
  7.2 60.9 %copy-start.20 = (s32[32]{0:T(128)S(1)}, s32[32]{0:T(128)}, u32[]{:S(2)}) copy-start(s32[32]{0:T(128)} %param.10) | copy-start | bytes 388
  7.2 61.2 %copy-start.21 = (s32[32]{0:T(128)S(1)}, s32[32]{0:T(128)}, u32[]{:S(2)}) copy-start(s32[32]{0:T(128)} %param.9) | copy-start | bytes 388
  7.2 494.8 %all-gather.3.cloned.1.call-start = ((), (), s32[]{:S(2)}) async-start(), calls=%async_computation | async-start | bytes 1622016 | tf_op jit(solution)/shard_map/all_gather | solution.py:86
  7.9 697.0 %all-gather.5.cloned.1.call-start = ((), (), s32[]{:S(2)}) async-start(), calls=%async_computation.1 | async-start | bytes 3244032 | tf_op jit(solution)/shard_map/all_gather | solution.py:110
  69.5 9.3 %copy-start.12 = (s32[2048]{0:T(1024)}, s32[2048]{0:T(1024)S(1)}, u32[]{:S(2)}) copy-start(s32[2048]{0:T(1024)S(1)} %broadcast_clamp_fusion) | copy-start | bytes 24580
  69.6 9.2 %copy-start.14 = (pred[2,1024]{1,0:T(4,128)(4,1)}, pred[2,1024]{1,0:T(4,128)(4,1)S(1)}, u32[]{:S(2)}) copy-start(pred[2,1024]{1,0:T(4,128)(4,1)S(1)} %get-tuple-element.251) | copy-start | bytes 6148
  69.6 9.2 %copy-start.16 = (pred[2,1024]{1,0:T(4,128)(4,1)}, pred[2,1024]{1,0:T(4,128)(4,1)S(1)}, u32[]{:S(2)}) copy-start(pred[2,1024]{1,0:T(4,128)(4,1)S(1)} %get-tuple-element.252) | copy-start | bytes 6148
  89.6 3.2 copy-start
  116.3 78.0 %copy-start.5 = (f32[2,128,128]{2,1,0:T(8,128)}, f32[2,128,128]{2,1,0:T(8,128)S(1)}, u32[]{:S(2)}) copy-start(f32[2,128,128]{2,1,0:T(8,128)S(1)} %custom-call.81) | copy-start | bytes 393220
  145.5 0.9 copy-start.1
  170.4 133.2 %copy-start.7 = (f32[2,128,128]{2,1,0:T(8,128)}, f32[2,128,128]{2,1,0:T(8,128)S(1)}, u32[]{:S(2)}) copy-start(f32[2,128,128]{2,1,0:T(8,128)S(1)} %custom-call.83) | copy-start | bytes 393220
  197.5 0.9 copy-start.2
  222.0 129.6 %copy-start.8 = (f32[2,128,128]{2,1,0:T(8,128)}, f32[2,128,128]{2,1,0:T(8,128)S(1)}, u32[]{:S(2)}) copy-start(f32[2,128,128]{2,1,0:T(8,128)S(1)} %custom-call.85) | copy-start | bytes 393220
  249.5 0.9 copy-start.3
  275.5 76.2 %copy-start.9 = (f32[2,128,128]{2,1,0:T(8,128)}, f32[2,128,128]{2,1,0:T(8,128)S(1)}, u32[]{:S(2)}) copy-start(f32[2,128,128]{2,1,0:T(8,128)S(1)} %custom-call.87) | copy-start | bytes 393220
  303.6 0.8 copy-start.4
  329.3 22.3 %copy-start.10 = (f32[2,128,128]{2,1,0:T(8,128)}, f32[2,128,128]{2,1,0:T(8,128)S(1)}, u32[]{:S(2)}) copy-start(f32[2,128,128]{2,1,0:T(8,128)S(1)} %custom-call.89) | copy-start | bytes 393220
  408.0 81.8 %copy-start.6 = (f32[2,128,128]{2,1,0:T(8,128)S(1)}, f32[2,128,128]{2,1,0:T(8,128)}, u32[]{:S(2)}) copy-start(f32[2,128,128]{2,1,0:T(8,128)} %copy-done.5) | copy-start | bytes 393220
  493.1 8.9 %copy-start.11 = (f32[64,384]{1,0:T(8,128)S(1)}, f32[64,384]{1,0:T(8,128)}, u32[]{:S(2)}) copy-start(f32[64,384]{1,0:T(8,128)} %custom-call.100) | copy-start | bytes 294916
  502.0 201.3 %copy-start.19 = (s32[2]{0:T(128)S(1)}, s32[2]{0:T(128)}, u32[]{:S(2)}) copy-start(s32[2]{0:T(128)} %get-tuple-element.181) | copy-start | bytes 28
  502.0 202.9 %copy-start.13 = (s32[2048]{0:T(1024)S(1)}, s32[2048]{0:T(1024)}, u32[]{:S(2)}) copy-start(s32[2048]{0:T(1024)} %copy-done.12) | copy-start | bytes 24580
  502.0 211.0 %copy-start.15 = (pred[2,1024]{1,0:T(4,128)(4,1)S(1)}, pred[2,1024]{1,0:T(4,128)(4,1)}, u32[]{:S(2)}) copy-start(pred[2,1024]{1,0:T(4,128)(4,1)} %copy-done.14) | copy-start | bytes 6148
  502.0 211.0 %copy-start.17 = (pred[2,1024]{1,0:T(4,128)(4,1)S(1)}, pred[2,1024]{1,0:T(4,128)(4,1)}, u32[]{:S(2)}) copy-start(pred[2,1024]{1,0:T(4,128)(4,1)} %copy-done.16) | copy-start | bytes 6148
Sparse Core Ops, SparseCore 0:
  10.8 59.4 all-gather.2
  523.0 56.2 all-gather.4
where the time goes:
time: 793 us; the launch traced here: 782 us
  other arithmetic  579 us (73%)
  matrix products  70.2 us (9%)
  local copies, waits for them, and re-layouts  60.4 us (8%)
  blocking collectives  55.7 us (7%)
  between operations  15.2 us (2%)
    another operation x34, other arithmetic, coupling(): diagonal_cholesky_factor = jnp.linalg.cholesky(dmat)  347 us
    another operation x9, other arithmetic, lower_triangular_solver(): lax.linalg.triangular_solve(factor, rhs, left_side=True, lower=True, tran...  186 us
    all_gather x1, blocking collectives, shards(): lax.all_gather(points, ('row', 'col'), axis=1, tiled=True)  55.7 us
    another operation x14, matrix products, coupling(): diagonal_cholesky_factor = jnp.linalg.cholesky(dmat)  38.7 us
    another operation x26, local copies, waits for them, and re-layouts  23.2 us
  transfers between devices with their start and end apart: 2, of which 0 were waited for; matrix products, arithmetic and copies ran while one was open for 78% of the time, Pallas kernels for 0%

commit v1 on v0

v1 whole, which is shorter than its diff:
```python
import functools
import math

import jax
import jax.numpy as jnp
from jax import lax
from jax.experimental import pallas as pl
from jax.experimental.pallas import tpu as pltpu
from jax.sharding import PartitionSpec as P

LEAF_MIN = 256
LEAF_MAX = 1024
SLOTS = 2
GAMMA = 8.0
SHIFT = 1.0
AMPC = 4.0

FEAT = 16
WINDOW = LEAF_MAX + 256
MAX_STEPS = 96
TOL = 1e-4
MESH = pl.DeviceIdType.MESH
VMEM = pltpu.MemorySpace.VMEM
SMEM = pltpu.MemorySpace.SMEM
F32 = jnp.float32
BF16 = jnp.bfloat16
SCALE = GAMMA * math.log2(math.e)


def three(value):
    high = value.astype(BF16).astype(F32)
    rest = value - high
    middle = rest.astype(BF16).astype(F32)
    low = (rest - middle).astype(BF16).astype(F32)
    return high, middle, low


def stack_rows(rows, width):
    ids = lax.broadcasted_iota(jnp.int32, (FEAT, width), 0)
    out = jnp.zeros((FEAT, width), F32)
    for spot, row in enumerate(rows):
        out = jnp.where(ids == spot, row, out)
    return out


def squares(p0, p1, p2):
    return p0 * p0 + p1 * p1 + p2 * p2


def left_features(p0, p1, p2):
    one = jnp.ones_like(p0)
    norms = three(-SCALE * squares(p0, p1, p2))
    return stack_rows([p0, p1, p2] * 3 + list(norms) + [one] * 3, p0.shape[1])


def right_features(p0, p1, p2, amp, valid):
    one = jnp.ones_like(p0)
    parts = [three(2.0 * SCALE * p) for p in (p0, p1, p2)]
    norm = math.log2(amp) - SCALE * squares(p0, p1, p2)
    if valid is not None:
        norm = jnp.where(valid, norm, -30000.0)
    rows = [parts[d][k] for k in range(3) for d in range(3)]
    return stack_rows(rows + [one] * 3 + list(three(norm)), p0.shape[1])


def fill_pack(omega_ref, pts_ref, dst):
    ranks = omega_ref.shape[0]
    pts = pts_ref[...].astype(F32)
    dst[0:ranks, :] = omega_ref[...]
    dst[ranks:ranks + FEAT, :] = left_features(pts[0:1], pts[1:2], pts[2:3]).astype(BF16)


def spread(block, send_sem, recv_sem):
    z, col = lax.axis_index("row"), lax.axis_index("col")
    y, x, core = col // 4, (col // 2) % 2, col % 2

    def at(zz, yy, xx, cc):
        return zz * 8 + yy * 4 + xx * 2 + cc

    zs = [lax.rem(z + d, 4) for d in range(4)]
    xn, yn, cn = (z, y * 4 + (1 - x) * 2 + core), (z, (1 - y) * 4 + x * 2 + core), (z, y * 4 + x * 2 + 1 - core)
    peers = [(zs[d], col) for d in (1, 3, 2)] + [xn, yn, cn]
    barrier = pltpu.get_barrier_semaphore()
    for peer in peers:
        pl.semaphore_signal(barrier, inc=1, device_id=peer, device_id_type=MESH)
    pl.semaphore_wait(barrier, len(peers))
    sent = []

    def send(index, to):
        copy = pltpu.make_async_remote_copy(
            src_ref=block(index), dst_ref=block(index),
            send_sem=send_sem.at[len(sent)], recv_sem=recv_sem.at[index],
            device_id=to, device_id_type=MESH,
        )
        copy.start()
        sent.append(copy)

    def receive(index):
        pltpu.make_async_remote_copy(
            src_ref=block(index), dst_ref=block(index),
            send_sem=send_sem.at[0], recv_sem=recv_sem.at[index],
            device_id=cn, device_id_type=MESH,
        ).wait_recv()

    mine = at(z, y, x, core)
    for peer in (xn, yn) + tuple(peers[:3]) + (cn,):
        send(mine, peer)
    for d in (1, 3, 2):
        got = at(zs[d], y, x, core)
        receive(got)
        for peer in (xn, yn, cn):
            send(got, peer)
    for d in (0, 1, 3, 2):
        via_x = at(zs[d], y, 1 - x, core)
        receive(via_x)
        if d < 2:
            send(via_x, yn)
        send(via_x, cn)
        via_y = at(zs[d], 1 - y, x, core)
        receive(via_y)
        if d >= 2:
            send(via_y, xn)
        send(via_y, cn)
    for d in (0, 1, 3, 2):
        far = at(zs[d], 1 - y, 1 - x, core)
        receive(far)
        send(far, cn)
    for d in (0, 1, 3, 2):
        receive(at(zs[d], y, x, 1 - core))
    for d in (0, 1, 3, 2):
        receive(at(zs[d], y, 1 - x, 1 - core))
        receive(at(zs[d], 1 - y, x, 1 - core))
    for d in (0, 1, 3, 2):
        receive(at(zs[d], 1 - y, 1 - x, 1 - core))
    for copy in sent:
        copy.wait_send()


def gather_pack_kernel(omega_ref, pts_ref, out_ref, send_sem, recv_sem):
    width = omega_ref.shape[1]

    def block(index):
        return out_ref.at[:, pl.ds(pl.multiple_of(index * width, 128), width)]

    device = lax.axis_index("row") * 8 + lax.axis_index("col")
    fill_pack(omega_ref, pts_ref, block(device))
    spread(block, send_sem, recv_sem)


def pack_kernel(omega_ref, pts_ref, out_ref):
    fill_pack(omega_ref, pts_ref, out_ref)


def owned(owner_ref, device, slot):
    seen, leaf = jnp.int32(0), jnp.int32(-1)
    for index in range(owner_ref.shape[0]):
        hit = (owner_ref[index] == device).astype(jnp.int32)
        take = hit * (seen == slot).astype(jnp.int32)
        leaf = leaf + take * (index - leaf)
        seen = seen + hit
    return leaf


def gather_coupling_kernel(owner_ref, block_ref, out_ref, buf, send_sem, recv_sem):
    device = lax.axis_index("row") * 8 + lax.axis_index("col")
    buf[device] = block_ref[...]
    spread(lambda index: buf.at[index], send_sem, recv_sem)
    for slot in range(SLOTS):
        leaf = owned(owner_ref, device, slot)
        found = buf[jnp.maximum(leaf, 0)]
        out_ref[slot] = jnp.where(leaf >= 0, found, 0.0)


def pick_kernel(where_ref, owner_ref, every_ref, out_ref):
    for slot in range(SLOTS):
        leaf = owned(owner_ref, where_ref[0], slot)
        found = every_ref[jnp.maximum(leaf, 0)]
        out_ref[slot] = jnp.where(leaf >= 0, found, 0.0)


def rolled(window, shift):
    return pltpu.roll(window, WINDOW - shift, 1)


def leaf_kernel(where_ref, extra_ref, g_ref, samp_ref, coup_ref, q_ref, acc_ref, k_ref, x_ref, r_ref, p_ref, *, amp, per_dev):
    ranks, total = samp_ref.shape[0], g_ref.shape[1]
    device = where_ref[0]

    def scan(index, carry):
        begin, size = carry
        now = extra_ref[index] + (LEAF_MIN - 1)
        begin = begin + jnp.where(index < device, now, 0)
        return begin, jnp.where(index == device, now, size)

    start, size = lax.fori_loop(0, extra_ref.shape[0], scan, (jnp.int32(0), jnp.int32(0)))
    base = pl.multiple_of(jnp.minimum((start // 128) * 128, total - WINDOW), 128)
    shift = start - base
    own = pl.multiple_of(device * per_dev, 128)

    valid = lax.broadcasted_iota(jnp.int32, (1, LEAF_MAX), 1) < size
    pts = rolled(g_ref[ranks:ranks + FEAT, pl.ds(base, WINDOW)].astype(F32), shift)[:, :LEAF_MAX]
    feats = right_features(pts[0:1], pts[1:2], pts[2:3], amp, valid)
    q_ref[0:LEAF_MAX, :] = feats.T.astype(BF16)
    leaf_left = left_features(pts[0:1], pts[1:2], pts[2:3])
    leaf_left = jnp.where(valid, leaf_left, 0.0)
    ids = lax.broadcasted_iota(jnp.int32, (FEAT, LEAF_MAX), 0)
    leaf_left = jnp.where(valid | (ids != 9), leaf_left, -30000.0).astype(BF16)
    mine = g_ref[ranks:ranks + FEAT, pl.ds(own, per_dev)].astype(F32)
    feats = right_features(mine[0:1], mine[1:2], mine[2:3], amp, None)
    q_ref[LEAF_MAX:LEAF_MAX + per_dev, :] = feats.T.astype(BF16)

    acc_ref[...] = jnp.zeros_like(acc_ref)
    count = LEAF_MAX + per_dev
    chunk = 512

    def step(outer, carry):
        at = pl.multiple_of(outer * chunk, 128)
        left = g_ref[ranks:ranks + FEAT, pl.ds(at, chunk)]
        omega = g_ref[0:ranks, pl.ds(at, chunk)]
        for low in range(0, count, 256):
            high = min(low + 256, count)
            power = jnp.dot(q_ref[low:high, :], left, preferred_element_type=F32)
            tile = jnp.exp2(power).astype(BF16)
            acc_ref[:, low:high] += lax.dot_general(
                omega, tile, (((1,), (1,)), ((), ())), preferred_element_type=F32)
        return carry

    lax.fori_loop(0, total // chunk, step, 0)

    mine = g_ref[0:ranks, pl.ds(own, per_dev)].astype(F32)
    samp_ref[...] = (acc_ref[:, LEAF_MAX:] + SHIFT * mine).astype(BF16)
    mine = rolled(g_ref[0:ranks, pl.ds(base, WINDOW)].astype(F32), shift)[:, :LEAF_MAX]
    y16 = jnp.where(valid, acc_ref[:, :LEAF_MAX] + SHIFT * mine, 0.0).astype(BF16)
    ys = y16.astype(F32)

    for low in range(0, LEAF_MAX, 256):
        power = jnp.dot(q_ref[low:low + 256, :], leaf_left, preferred_element_type=F32)
        k_ref[low:low + 256, :] = jnp.exp2(power).astype(BF16)

    x_ref[...] = jnp.zeros_like(x_ref)
    r_ref[...] = ys
    p_ref[...] = ys
    norm0 = jnp.sum(ys * ys, axis=1, keepdims=True)

    def going(carry):
        index, worst, _ = carry
        return (index < MAX_STEPS) & (worst > TOL * TOL)

    def iterate(carry):
        index, _, norm = carry
        p = p_ref[...]
        high = p.astype(BF16)
        low = (p - high.astype(F32)).astype(BF16)
        both = jnp.dot(jnp.concatenate([high, low], axis=0), k_ref[...], preferred_element_type=F32)
        dp = SHIFT * p + both[:ranks] + both[ranks:]
        energy = jnp.sum(p * dp, axis=1, keepdims=True)
        alpha = jnp.where(energy > 0.0, norm / energy, 0.0)
        x_ref[...] += alpha * p
        r = r_ref[...] - alpha * dp
        r_ref[...] = r
        fresh = jnp.sum(r * r, axis=1, keepdims=True)
        p_ref[...] = r + jnp.where(norm > 0.0, fresh / norm, 0.0) * p
        worst = jnp.max(jnp.where(norm0 > 0.0, fresh / norm0, 0.0))
        return index + 1, worst, fresh

    lax.while_loop(going, iterate, (jnp.int32(0), F32(1.0), norm0))

    nt = (((1,), (1,)), ((), ()))
    exact = dict(precision=lax.Precision.HIGHEST, preferred_element_type=F32)
    x = x_ref[...]
    inner = lax.dot_general(ys, x, nt, **exact) + lax.dot_general(x, r_ref[...], nt, **exact)
    gram = lax.dot_general(y16, y16, nt, preferred_element_type=F32)
    rows = lax.broadcasted_iota(jnp.int32, (ranks, 1), 0)
    cols = lax.broadcasted_iota(jnp.int32, (1, ranks), 1)
    eye = jnp.where(rows == cols, 1.0, 0.0).astype(F32)

    left = jnp.concatenate([inner, eye], axis=1)
    right = gram
    dinv = jnp.ones((ranks, 1), F32)
    root = jnp.ones((ranks, 1), F32)
    for k in range(ranks):
        a, b = left[k:k + 1, :], right[k:k + 1, :]
        ainv, binv = 1.0 / a[:, k:k + 1], 1.0 / b[:, k:k + 1]
        below = rows > k
        left = left - jnp.where(below, left[:, k:k + 1] * ainv, 0.0) * a
        right = right - jnp.where(below, right[:, k:k + 1] * binv, 0.0) * b
        dinv = jnp.where(rows == k, ainv, dinv)
        root = jnp.where(rows == k, jnp.sqrt(binv), root)
    upper = jnp.where(cols >= rows, right * root, 0.0)
    mid = lax.dot_general(left[:, ranks:], upper, nt, **exact)
    coup = lax.dot_general(mid, mid * dinv, (((0,), (0,)), ((), ())), **exact)
    half = ranks // 2
    coup_ref[:, :ranks] = coup[:half]
    coup_ref[:, ranks:] = coup[half:]


def shards(points, omega, leaf_extra, owner_map):
    ranks, per_dev = omega.shape
    n_row, n_col = lax.axis_size("row"), lax.axis_size("col")
    n_dev = n_row * n_col
    n_all = per_dev * n_dev
    amp = AMPC / math.sqrt(n_all)
    device = lax.axis_index(("row", "col"))
    block = (ranks // 2, 2 * ranks)
    small = (n_row, n_col) == (4, 8)
    vm = pl.BlockSpec(memory_space=VMEM)
    sm = pl.BlockSpec(memory_space=SMEM)
    sems = [pltpu.SemaphoreType.DMA((31,)), pltpu.SemaphoreType.DMA((32,))]
    if small:
        pack = pl.pallas_call(
            gather_pack_kernel,
            out_shape=jax.ShapeDtypeStruct((ranks + FEAT, n_all), BF16),
            in_specs=[vm, vm], out_specs=vm, scratch_shapes=sems,
            compiler_params=pltpu.CompilerParams(collective_id=0, has_side_effects=True, vmem_limit_bytes=24 << 20),
        )(omega, points)
    else:
        pack = pl.pallas_call(
            pack_kernel,
            out_shape=jax.ShapeDtypeStruct((ranks + FEAT, per_dev), BF16),
            in_specs=[vm, vm], out_specs=vm,
        )(omega, points)
        pack = lax.all_gather(pack, ("row", "col"), axis=1, tiled=True)
    samples, coup = pl.pallas_call(
        functools.partial(leaf_kernel, amp=amp, per_dev=per_dev),
        out_shape=(jax.ShapeDtypeStruct((ranks, per_dev), BF16), jax.ShapeDtypeStruct(block, F32)),
        in_specs=[sm, sm, vm], out_specs=(vm, vm),
        scratch_shapes=[
            pltpu.VMEM((LEAF_MAX + per_dev, FEAT), BF16),
            pltpu.VMEM((ranks, LEAF_MAX + per_dev), F32),
            pltpu.VMEM((LEAF_MAX, LEAF_MAX), BF16),
            pltpu.VMEM((ranks, LEAF_MAX), F32),
            pltpu.VMEM((ranks, LEAF_MAX), F32),
            pltpu.VMEM((ranks, LEAF_MAX), F32),
        ],
        compiler_params=pltpu.CompilerParams(vmem_limit_bytes=48 << 20),
    )(device.astype(jnp.int32).reshape(1), leaf_extra, pack)
    if small:
        mine = pl.pallas_call(
            gather_coupling_kernel,
            out_shape=jax.ShapeDtypeStruct((SLOTS,) + block, F32),
            in_specs=[sm, vm], out_specs=vm,
            scratch_shapes=[pltpu.VMEM((n_dev,) + block, F32)] + sems,
            compiler_params=pltpu.CompilerParams(collective_id=1, has_side_effects=True),
        )(owner_map, coup)
    else:
        every = lax.all_gather(coup, ("row", "col"), axis=0)
        mine = pl.pallas_call(
            pick_kernel,
            out_shape=jax.ShapeDtypeStruct((SLOTS,) + block, F32),
            in_specs=[sm, sm, vm], out_specs=vm,
        )(device.astype(jnp.int32).reshape(1), owner_map, every)
    coupled = mine.reshape(SLOTS, ranks // 2, 2, ranks).transpose(0, 2, 1, 3).reshape(SLOTS, ranks * ranks)
    return samples, coupled


def solution(mesh):
    return jax.shard_map(
        shards,
        mesh=mesh,
        in_specs=(P(None, ("row", "col")), P(None, ("row", "col")), P(), P()),
        out_specs=(P(None, ("row", "col")), P(("row", "col"), None)),
        check_vma=False,
    )
```

time: 793 us -> 89.1 us (0.11); the launches traced: 782 us -> 88.8 us
  other arithmetic: 579 us -> 0 us
  Pallas kernels: 0 us -> 84.4 us
  matrix products: 70.2 us -> 0 us
  local copies, waits for them, and re-layouts: 60.4 us -> 3.71 us
  blocking collectives: 55.7 us -> 0 us
  between operations: 15.2 us -> 0.69 us
    another operation x55 -> x0, other arithmetic: 557 us -> none  [the longest x34 347 us: coupling(): diagonal_cholesky_factor = jnp.linalg.cholesky(dmat)]
    pallas_call x0 -> x3, Pallas kernels: none -> 84.4 us  [the longest x1 48.2 us: shards(): pl.pallas_call(functools.partial(leaf_kernel, amp=amp, per_dev=per_dev),...]
    all_gather x1 -> x0, blocking collectives: 55.7 us -> none  [shards(): lax.all_gather(points, ('row', 'col'), axis=1, tiled=True)]
    another operation x32 -> x0, matrix products: 54.2 us -> none  [the longest x14 38.7 us: coupling(): diagonal_cholesky_factor = jnp.linalg.cholesky(dmat)]
    another operation x35 -> x0, local copies, waits for them, and re-layouts: 30.1 us -> none
    gather x4 -> x0, local copies, waits for them, and re-layouts: 17.3 us -> none  [the longest x2 9.21 us: shards(): jnp.take(piece_pts, spot, axis=1)]
    dot_general x8 -> x0, matrix products: 15.9 us -> none  [the longest x6 15.1 us: row_step(): term = jnp.dot(comega, tile, preferred_element_type=jnp.float32)]
    div x3 -> x0, other arithmetic: 10.7 us -> none  [the longest x1 10.7 us: coupling(): diagonal_cholesky_factor = jnp.linalg.cholesky(dmat)]
  transfers between devices with their start and end apart: 2 -> 0, of which waited for: 0 -> 0; matrix products, arithmetic and copies ran while one was open for 78% -> 0% of each run, Pallas kernels for 0% -> 0%
where the time goes in v1:
time: 89.1 us; the launch traced here: 88.8 us
  Pallas kernels  84.4 us (95%)
  local copies, waits for them, and re-layouts  3.71 us (4%)
    pallas_call x1, Pallas kernels, shards(): pl.pallas_call(functools.partial(leaf_kernel, amp=amp, per_dev=per_dev),...  48.2 us
    pallas_call x1, Pallas kernels, shards(): pl.pallas_call(gather_pack_kernel, out_shape=jax.ShapeDtypeStruct((ranks...  20.8 us
    pallas_call x1, Pallas kernels, shards(): pl.pallas_call(gather_coupling_kernel, out_shape=jax.ShapeDtypeStruct((SL...  15.4 us
    unnamed x8, local copies, waits for them, and re-layouts  2.14 us

profile of v1, /device:TPU:0, one launch (start us, length us, event | category | flops | bytes accessed | tf_op | source)
XLA Modules:
  0.0 88.8 jit_solution(11149012913102208261)
XLA Ops:
  0.6 0.0 copy-start.3
  0.6 0.0 copy-start
  0.7 0.8 copy-done
  1.4 0.0 copy-start.2
  1.4 0.7 copy-done.2
  2.1 20.8 %shard_map.59.g_ref = bf16[80,12288]{1,0:T(8,128)(2,1)S(1)} custom-call(bf16[64,384]{1,0:T(8,128)(2,1)S(1)} %copy-done, bf16[3,384]{1,0:T(4,128)(2,1)S(1)} %copy-done.2), custom_call_target="tpu_custom_call" | custom-call | tf_op jit(solution)/shard_map/pallas_call | solution.py:310
  23.0 0.0 copy-done.3
  23.0 48.2 %shard_map.60 = (bf16[64,384]{1,0:T(8,128)(2,1)}, f32[32,128]{1,0:T(8,128)S(1)}) custom-call(s32[1]{0:T(128)} %bitcast.where_ref, s32[32]{0:T(128)S(1)} %copy-done.3, bf16[80,12288]{1,0:T(8,128)(2,1)S(1)} %shard_map.59.g_ref), custom_call_target="tpu_custom_call" | custom-call | tf_op jit(solution)/shard_map/pallas_call | solution.py:323
  71.2 0.0 copy-start.1
  71.2 0.7 copy-done.1
  71.8 15.4 %shard_map.61 = f32[2,32,128]{2,1,0:T(8,128)} custom-call(s32[32]{0:T(128)} %owner_ref.1, f32[32,128]{1,0:T(8,128)} %copy-done.1), custom_call_target="tpu_custom_call" | custom-call | tf_op jit(solution)/shard_map/pallas_call | solution.py:338
  87.2 0.9 reshape.14
  88.1 0.7 reshape.15
  (1 shorter events, 0.0 us)
Async XLA Ops:
  0.6 22.4 %copy-start.3 = (s32[32]{0:T(128)S(1)}, s32[32]{0:T(128)}, u32[]{:S(2)}) copy-start(s32[32]{0:T(128)} %extra_ref.1) | copy-start | bytes 388
  0.6 0.8 copy-start
  1.4 0.7 copy-start.2
  71.2 0.7 copy-start.1

commit v2 on v1

v2 whole, which is shorter than its diff:
```python
import functools
import math

import jax
import jax.numpy as jnp
from jax import lax
from jax.experimental import pallas as pl
from jax.experimental.pallas import tpu as pltpu
from jax.sharding import PartitionSpec as P

LEAF_MIN = 256
LEAF_MAX = 1024
SLOTS = 2
GAMMA = 8.0
SHIFT = 1.0
AMPC = 4.0

FEAT = 16
WINDOW = LEAF_MAX + 256
MAX_STEPS = 96
PART = 256
JCHUNK = 4096
TOL = 1e-4
MESH = pl.DeviceIdType.MESH
VMEM = pltpu.MemorySpace.VMEM
SMEM = pltpu.MemorySpace.SMEM
F32 = jnp.float32
BF16 = jnp.bfloat16
SCALE = GAMMA * math.log2(math.e)


def three(value):
    high = value.astype(BF16).astype(F32)
    rest = value - high
    middle = rest.astype(BF16).astype(F32)
    low = (rest - middle).astype(BF16).astype(F32)
    return high, middle, low


def stack_rows(rows, width):
    ids = lax.broadcasted_iota(jnp.int32, (FEAT, width), 0)
    out = jnp.zeros((FEAT, width), F32)
    for spot, row in enumerate(rows):
        out = jnp.where(ids == spot, row, out)
    return out


def squares(p0, p1, p2):
    return p0 * p0 + p1 * p1 + p2 * p2


def left_features(p0, p1, p2):
    one = jnp.ones_like(p0)
    norms = three(-SCALE * squares(p0, p1, p2))
    return stack_rows([p0, p1, p2] * 3 + list(norms) + [one] * 3, p0.shape[1])


def right_features(p0, p1, p2, amp, valid):
    one = jnp.ones_like(p0)
    parts = [three(2.0 * SCALE * p) for p in (p0, p1, p2)]
    norm = math.log2(amp) - SCALE * squares(p0, p1, p2)
    if valid is not None:
        norm = jnp.where(valid, norm, -30000.0)
    rows = [parts[d][k] for k in range(3) for d in range(3)]
    return stack_rows(rows + [one] * 3 + list(three(norm)), p0.shape[1])


def fill_pack(omega_ref, pts_ref, dst):
    ranks = omega_ref.shape[0]
    pts = pts_ref[...].astype(F32)
    dst[0:ranks, :] = omega_ref[...]
    dst[ranks:ranks + FEAT, :] = left_features(pts[0:1], pts[1:2], pts[2:3]).astype(BF16)


def spread(block, send_sem, recv_sem):
    z, col = lax.axis_index("row"), lax.axis_index("col")
    y, x, core = col // 4, (col // 2) % 2, col % 2

    def at(zz, yy, xx, cc):
        return zz * 8 + yy * 4 + xx * 2 + cc

    zs = [lax.rem(z + d, 4) for d in range(4)]
    xn, yn, cn = (z, y * 4 + (1 - x) * 2 + core), (z, (1 - y) * 4 + x * 2 + core), (z, y * 4 + x * 2 + 1 - core)
    peers = [(zs[d], col) for d in (1, 3, 2)] + [xn, yn, cn]
    barrier = pltpu.get_barrier_semaphore()
    for peer in peers:
        pl.semaphore_signal(barrier, inc=1, device_id=peer, device_id_type=MESH)
    pl.semaphore_wait(barrier, len(peers))
    sent = []

    def send(index, to):
        copy = pltpu.make_async_remote_copy(
            src_ref=block(index), dst_ref=block(index),
            send_sem=send_sem.at[len(sent)], recv_sem=recv_sem.at[index],
            device_id=to, device_id_type=MESH,
        )
        copy.start()
        sent.append(copy)

    def receive(index):
        pltpu.make_async_remote_copy(
            src_ref=block(index), dst_ref=block(index),
            send_sem=send_sem.at[0], recv_sem=recv_sem.at[index],
            device_id=cn, device_id_type=MESH,
        ).wait_recv()

    mine = at(z, y, x, core)
    for peer in (xn, yn) + tuple(peers[:3]) + (cn,):
        send(mine, peer)
    for d in (1, 3, 2):
        got = at(zs[d], y, x, core)
        receive(got)
        for peer in (xn, yn, cn):
            send(got, peer)
    for d in (0, 1, 3, 2):
        via_x = at(zs[d], y, 1 - x, core)
        receive(via_x)
        if d < 2:
            send(via_x, yn)
        send(via_x, cn)
        via_y = at(zs[d], 1 - y, x, core)
        receive(via_y)
        if d >= 2:
            send(via_y, xn)
        send(via_y, cn)
    for d in (0, 1, 3, 2):
        far = at(zs[d], 1 - y, 1 - x, core)
        receive(far)
        send(far, cn)
    for d in (0, 1, 3, 2):
        receive(at(zs[d], y, x, 1 - core))
    for d in (0, 1, 3, 2):
        receive(at(zs[d], y, 1 - x, 1 - core))
        receive(at(zs[d], 1 - y, x, 1 - core))
    for d in (0, 1, 3, 2):
        receive(at(zs[d], 1 - y, 1 - x, 1 - core))
    for copy in sent:
        copy.wait_send()


def gather_pack_kernel(omega_ref, pts_ref, out_ref, send_sem, recv_sem):
    width = omega_ref.shape[1]

    def block(index):
        return out_ref.at[:, pl.ds(pl.multiple_of(index * width, 128), width)]

    device = lax.axis_index("row") * 8 + lax.axis_index("col")
    fill_pack(omega_ref, pts_ref, block(device))
    spread(block, send_sem, recv_sem)


def pack_kernel(omega_ref, pts_ref, out_ref):
    fill_pack(omega_ref, pts_ref, out_ref)


def rolled(window, shift):
    return pltpu.roll(window, WINDOW - shift, 1)


def slots_of(owner_ref, extra_ref, device):
    def scan(index, carry):
        begin, seen, found = carry
        size = extra_ref[index] + (LEAF_MIN - 1)
        hit = owner_ref[index] == device
        found = tuple(
            (jnp.where(hit & (seen == slot), begin, old[0]), jnp.where(hit & (seen == slot), size, old[1]))
            for slot, old in enumerate(found)
        )
        return begin + size, seen + hit.astype(jnp.int32), found

    zero = jnp.int32(0)
    return lax.fori_loop(0, owner_ref.shape[0], scan, (zero, zero, ((zero, zero),) * SLOTS))[2]


def leaf_kernel(where_ref, owner_ref, extra_ref, g_ref, samp_ref, coup_ref, q_ref, left_ref, turned_ref, acc_ref, k_ref,
                x_ref, r_ref, p_ref, inner_ref, gram_ref, out_ref, *, amp, per_dev):
    ranks, total = samp_ref.shape[0], g_ref.shape[1]
    device = where_ref[0]
    leaves = slots_of(owner_ref, extra_ref, device)
    own = pl.multiple_of(device * per_dev, 128)
    own_at = SLOTS * LEAF_MAX
    nt = (((1,), (1,)), ((), ()))
    exact = dict(precision=lax.Precision.HIGHEST, preferred_element_type=F32)

    def window(slot):
        start, size = leaves[slot]
        base = pl.multiple_of(jnp.minimum((start // 128) * 128, total - WINDOW), 128)
        return base, start - base, lax.broadcasted_iota(jnp.int32, (1, LEAF_MAX), 1) < size

    for slot in range(SLOTS):
        @pl.when(leaves[slot][1] > 0)
        def _():
            base, shift, valid = window(slot)
            pts = rolled(g_ref[ranks:ranks + FEAT, pl.ds(base, WINDOW)].astype(F32), shift)[:, :LEAF_MAX]
            feats = right_features(pts[0:1], pts[1:2], pts[2:3], amp, valid)
            q_ref[:, slot * LEAF_MAX:(slot + 1) * LEAF_MAX] = feats.astype(BF16)
            mirror = jnp.where(valid, left_features(pts[0:1], pts[1:2], pts[2:3]), 0.0)
            ids = lax.broadcasted_iota(jnp.int32, (FEAT, LEAF_MAX), 0)
            left_ref[slot] = jnp.where(valid | (ids != 9), mirror, -30000.0).T.astype(BF16)

    mine = g_ref[ranks:ranks + FEAT, pl.ds(own, per_dev)].astype(F32)
    feats = right_features(mine[0:1], mine[1:2], mine[2:3], amp, None)
    q_ref[:, own_at:own_at + per_dev] = feats.astype(BF16)

    chunk = math.gcd(total, JCHUNK)

    def sample(points):
        def step(outer, acc):
            at = pl.multiple_of(outer * chunk, 128)
            power = jnp.dot(turned_ref[pl.ds(at, chunk), :], points, preferred_element_type=F32)
            tile = jnp.exp2(power).astype(BF16)
            return acc + jnp.dot(g_ref[0:ranks, pl.ds(at, chunk)], tile, preferred_element_type=F32)

        return lax.fori_loop(0, total // chunk, step, jnp.zeros((ranks, points.shape[1]), F32))

    turn = math.gcd(total, 1024)

    def transpose(index, carry):
        at = pl.multiple_of(index * turn, 128)
        turned_ref[pl.ds(at, turn), :] = g_ref[ranks:ranks + FEAT, pl.ds(at, turn)].astype(F32).T.astype(BF16)
        return carry

    lax.fori_loop(0, total // turn, transpose, 0)

    mine = g_ref[0:ranks, pl.ds(own, per_dev)].astype(F32)
    samp_ref[...] = (sample(q_ref[:, own_at:own_at + per_dev]) + SHIFT * mine).astype(BF16)

    counts = [(leaves[slot][1] + PART - 1) // PART for slot in range(SLOTS)]

    def part(index, carry):
        at = jnp.where(index < counts[0], index * PART, LEAF_MAX + (index - counts[0]) * PART)
        at = pl.multiple_of(at, PART)
        acc_ref[:, pl.ds(at, PART)] = sample(q_ref[:, pl.ds(at, PART)])
        return carry

    lax.fori_loop(0, counts[0] + counts[1], part, 0)

    def solve(slot, n):
        base, shift, valid = window(slot)
        mine = rolled(g_ref[0:ranks, pl.ds(base, WINDOW)].astype(F32), shift)[:, :n]
        total_y = acc_ref[:, slot * LEAF_MAX:slot * LEAF_MAX + n] + SHIFT * mine
        y16 = jnp.where(valid[:, :n], total_y, 0.0).astype(BF16)
        ys = y16.astype(F32)

        for low in range(0, n, 256):
            q = q_ref[:, slot * LEAF_MAX:slot * LEAF_MAX + n]
            power = jnp.dot(left_ref[slot, low:low + 256, :], q, preferred_element_type=F32)
            k_ref[low:low + 256, :n] = jnp.exp2(power).astype(BF16)

        x_ref[:, :n] = jnp.zeros((ranks, n), F32)
        r_ref[:, :n] = ys
        p_ref[:, :n] = ys
        norm0 = jnp.sum(ys * ys, axis=1, keepdims=True)

        def going(carry):
            index, worst, _ = carry
            return (index < MAX_STEPS) & (worst > TOL * TOL)

        def iterate(carry):
            index, _, norm = carry
            p = p_ref[:, :n]
            high = p.astype(BF16)
            low = (p - high.astype(F32)).astype(BF16)
            both = jnp.dot(jnp.concatenate([high, low], axis=0), k_ref[:n, :n], preferred_element_type=F32)
            dp = SHIFT * p + both[:ranks] + both[ranks:]
            energy = jnp.sum(p * dp, axis=1, keepdims=True)
            alpha = jnp.where(energy > 0.0, norm / energy, 0.0)
            x_ref[:, :n] += alpha * p
            r = r_ref[:, :n] - alpha * dp
            r_ref[:, :n] = r
            fresh = jnp.sum(r * r, axis=1, keepdims=True)
            p_ref[:, :n] = r + jnp.where(norm > 0.0, fresh / norm, 0.0) * p
            worst = jnp.max(jnp.where(norm0 > 0.0, fresh / norm0, 0.0))
            return index + 1, worst, fresh

        lax.while_loop(going, iterate, (jnp.int32(0), F32(1.0), norm0))
        x = x_ref[:, :n]
        inner_ref[slot] = lax.dot_general(ys, x, nt, **exact) + lax.dot_general(x, r_ref[:, :n], nt, **exact)
        gram_ref[slot] = lax.dot_general(y16, y16, nt, preferred_element_type=F32)

    for slot in range(SLOTS):
        size = leaves[slot][1]
        for under, n in ((0, LEAF_MAX // 2), (LEAF_MAX // 2, LEAF_MAX)):
            @pl.when((size > under) & (size <= n))
            def _():
                solve(slot, n)

    coup_ref[...] = jnp.zeros_like(coup_ref)

    @pl.when(leaves[0][1] > 0)
    def _():
        rows = lax.broadcasted_iota(jnp.int32, (ranks, 1), 0)
        cols = lax.broadcasted_iota(jnp.int32, (1, ranks), 1)
        eye = jnp.where(rows == cols, 1.0, 0.0).astype(F32)
        state = [
            [jnp.concatenate([inner_ref[slot], eye], axis=1), gram_ref[slot], jnp.ones((ranks, 1), F32), jnp.ones((ranks, 1), F32)]
            for slot in range(SLOTS)
        ]
        for k in range(ranks):
            below = rows > k
            for item in state:
                left, right, dinv, root = item
                a, b = left[k:k + 1, :], right[k:k + 1, :]
                ainv, binv = 1.0 / a[:, k:k + 1], 1.0 / b[:, k:k + 1]
                item[0] = left - jnp.where(below, left[:, k:k + 1] * ainv, 0.0) * a
                item[1] = right - jnp.where(below, right[:, k:k + 1] * binv, 0.0) * b
                item[2] = jnp.where(rows == k, ainv, dinv)
                item[3] = jnp.where(rows == k, jnp.sqrt(binv), root)
        for slot, (left, right, dinv, root) in enumerate(state):
            @pl.when(leaves[slot][1] > 0)
            def _():
                upper = jnp.where(cols >= rows, right * root, 0.0)
                mid = lax.dot_general(left[:, ranks:], upper, nt, **exact)
                out_ref[...] = lax.dot_general(mid, mid * dinv, (((0,), (0,)), ((), ())), **exact)
                half = ranks // 2
                pairs = jnp.concatenate(
                    [out_ref[pl.ds(0, half, stride=2), :], out_ref[pl.ds(1, half, stride=2), :]], axis=1)
                for row in range(half):
                    at = row * 2 * ranks
                    coup_ref[slot:slot + 1, at:at + 2 * ranks] = pairs[row:row + 1, :]


def shards(points, omega, leaf_extra, owner_map):
    ranks, per_dev = omega.shape
    n_row, n_col = lax.axis_size("row"), lax.axis_size("col")
    n_dev = n_row * n_col
    n_all = per_dev * n_dev
    amp = AMPC / math.sqrt(n_all)
    device = lax.axis_index(("row", "col"))
    small = (n_row, n_col) == (4, 8)
    vm = pl.BlockSpec(memory_space=VMEM)
    sm = pl.BlockSpec(memory_space=SMEM)
    sems = [pltpu.SemaphoreType.DMA((31,)), pltpu.SemaphoreType.DMA((32,))]
    if small:
        pack = pl.pallas_call(
            gather_pack_kernel,
            out_shape=jax.ShapeDtypeStruct((ranks + FEAT, n_all), BF16),
            in_specs=[vm, vm], out_specs=vm, scratch_shapes=sems,
            compiler_params=pltpu.CompilerParams(collective_id=0, has_side_effects=True, vmem_limit_bytes=24 << 20),
        )(omega, points)
    else:
        pack = pl.pallas_call(
            pack_kernel,
            out_shape=jax.ShapeDtypeStruct((ranks + FEAT, per_dev), BF16),
            in_specs=[vm, vm], out_specs=vm,
        )(omega, points)
        pack = lax.all_gather(pack, ("row", "col"), axis=1, tiled=True)
    return pl.pallas_call(
        functools.partial(leaf_kernel, amp=amp, per_dev=per_dev),
        out_shape=(
            jax.ShapeDtypeStruct((ranks, per_dev), BF16),
            jax.ShapeDtypeStruct((SLOTS, ranks * ranks), F32),
        ),
        in_specs=[sm, sm, sm, vm], out_specs=(vm, vm),
        scratch_shapes=[
            pltpu.VMEM((FEAT, SLOTS * LEAF_MAX + per_dev), BF16),
            pltpu.VMEM((SLOTS, LEAF_MAX, FEAT), BF16),
            pltpu.VMEM((n_all, FEAT), BF16),
            pltpu.VMEM((ranks, SLOTS * LEAF_MAX), F32),
            pltpu.VMEM((LEAF_MAX, LEAF_MAX), BF16),
            pltpu.VMEM((ranks, LEAF_MAX), F32),
            pltpu.VMEM((ranks, LEAF_MAX), F32),
            pltpu.VMEM((ranks, LEAF_MAX), F32),
            pltpu.VMEM((SLOTS, ranks, ranks), F32),
            pltpu.VMEM((SLOTS, ranks, ranks), F32),
            pltpu.VMEM((ranks, ranks), F32),
        ],
        compiler_params=pltpu.CompilerParams(vmem_limit_bytes=48 << 20),
    )(device.astype(jnp.int32).reshape(1), owner_map, leaf_extra, pack)


def solution(mesh):
    return jax.shard_map(
        shards,
        mesh=mesh,
        in_specs=(P(None, ("row", "col")), P(None, ("row", "col")), P(), P()),
        out_specs=(P(None, ("row", "col")), P(("row", "col"), None)),
        check_vma=False,
    )
```

time: 89.1 us -> 73.3 us (0.82)
  the two profiles are of different devices: /device:TPU:0 before, /device:TPU:6 now
where the time goes in v2:
time: 73.3 us
  Pallas kernels  71.1 us (97%)
  local copies, waits for them, and re-layouts  1.49 us (2%)
    pallas_call x1, Pallas kernels, shards(): pl.pallas_call(functools.partial(leaf_kernel, amp=amp, per_dev=per_dev),...  52.7 us
    pallas_call x1, Pallas kernels, shards(): pl.pallas_call(gather_pack_kernel, out_shape=jax.ShapeDtypeStruct((ranks...  18.4 us
    unnamed x8, local copies, waits for them, and re-layouts  1.49 us

profile of v2, /device:TPU:6, one launch (start us, length us, event | category | flops | bytes accessed | tf_op | source)
XLA Modules:
  0.0 73.3 jit_solution(2196834337704746519)
XLA Ops:
  0.6 0.0 copy-start.2
  0.6 0.0 copy-start.3
  0.7 0.0 copy-start
  0.7 0.8 %copy-done = bf16[64,384]{1,0:T(8,128)(2,1)S(1)} copy-done((bf16[64,384]{1,0:T(8,128)(2,1)S(1)}, bf16[64,384]{1,0:T(8,128)(2,1)}, u32[]{:S(2)}) %copy-start) | copy-done | bytes 49176
  1.5 0.0 copy-start.1
  1.5 0.7 copy-done.1
  2.1 18.4 %shard_map.59.g_ref = bf16[80,12288]{1,0:T(8,128)(2,1)S(1)} custom-call(bf16[64,384]{1,0:T(8,128)(2,1)S(1)} %copy-done, bf16[3,384]{1,0:T(4,128)(2,1)S(1)} %copy-done.1), custom_call_target="tpu_custom_call" | custom-call | tf_op jit(solution)/shard_map/pallas_call | solution.py:335
  20.6 0.0 copy-done.2
  20.6 0.0 copy-done.3
  20.6 52.7 %shard_map.60 = (bf16[64,384]{1,0:T(8,128)(2,1)}, f32[2,4096]{1,0:T(2,128)}) custom-call(s32[1]{0:T(128)} %bitcast.where_ref, s32[32]{0:T(128)S(1)} %copy-done.2, s32[32]{0:T(128)S(1)} %copy-done.3, bf16[80,12288]{1,0:T(8,128)(2,1)S(1)} %shard_map.59.g_ref), custom_call_target="tpu_custom_call" | custom-call | tf_op jit(solution)/shard_map/pallas_call | solution.py:348
Async XLA Ops:
  0.6 19.9 %copy-start.2 = (s32[32]{0:T(128)S(1)}, s32[32]{0:T(128)}, u32[]{:S(2)}) copy-start(s32[32]{0:T(128)} %owner_ref.1) | copy-start | bytes 388
  0.6 19.9 %copy-start.3 = (s32[32]{0:T(128)S(1)}, s32[32]{0:T(128)}, u32[]{:S(2)}) copy-start(s32[32]{0:T(128)} %extra_ref.1) | copy-start | bytes 388
  0.7 0.8 %copy-start = (bf16[64,384]{1,0:T(8,128)(2,1)S(1)}, bf16[64,384]{1,0:T(8,128)(2,1)}, u32[]{:S(2)}) copy-start(bf16[64,384]{1,0:T(8,128)(2,1)} %omega_ref.1) | copy-start | bytes 147460
  1.5 0.7 copy-start.1
